TPU v7x, 512 devices: a whole 4x8x8 slice. The times are simulated.
512 devices in a mesh: users: 16 (over y_lo, x), items: 32 (over z, y_hi, core).
Axes of the slice: x: 4, y: 8 (y_hi: 2, y_lo: 4; y = y_hi * 4 + y_lo), z: 8, core: 2. Of those that a mesh axis runs over, the one named last changes fastest.
Arguments:
- histories: int32 [16, 256], replicated, may hold values from 0 to 1048575
- item_degree: int32 [1048576], P('items'), may hold values from 1 to 63
- user_degree: int32 [131072], P('users'), may hold values from 1 to 63
- tile_values: float32 [16, 32, 24, 128, 128], P('users', 'items'), may hold values from 0 to 1
- tile_rows: int32 [16, 32, 24], P('users', 'items'), may hold values from 0 to 63
- tile_cols: int32 [16, 32, 24], P('users', 'items'), may hold values from 0 to 255
- tile_count: int32 [16, 32], P('users', 'items'), may hold values from 1 to 24, as said below
Outputs:
- scores: float32 [16, 1048576], P('users', 'items')
Inputs may be any that keep to these rules, and one draw needn't show every extreme that they name: `tile_count`: every device has 1 to 24 live slots, and some device has exactly 24.
All inputs are finite; a program needn't handle non-finite values.
Results may differ from a plain program's by a relative error of at most 0.0003.
Values sent between devices are 32-bit elements; how exact they have to be, the bound alone decides.
A program may use at most 64 MiB of HBM per device.

v0:
```python
import jax
import jax.numpy as jnp
from jax import lax
from jax.sharding import PartitionSpec as P


def body(histories, item_degree, user_degree, tile_values, tile_rows, tile_cols, tile_count):
    highest = lax.Precision.HIGHEST
    queries = histories.shape[0]
    items_local = item_degree.shape[0]
    users_local = user_degree.shape[0]
    width = tile_values.shape[-1]
    item_blocks = items_local // width
    user_blocks = users_local // width
    values_now = tile_values[0, 0]
    block_rows = tile_rows[0, 0]
    block_cols = tile_cols[0, 0]
    slot_ids = jnp.arange(values_now.shape[0], dtype=jnp.int32)
    alive_mask = (slot_ids < tile_count[0, 0]).astype(jnp.float32)
    offset = lax.axis_index("items") * items_local
    local_ids = histories - offset
    inside = (local_ids >= 0) & (local_ids < items_local)
    query_ids = jnp.broadcast_to(jnp.arange(queries, dtype=jnp.int32)[:, None], histories.shape)
    hits = (
        jnp.zeros((queries, items_local), jnp.float32)
        .at[query_ids, jnp.clip(local_ids, 0, items_local - 1)]
        .add(jnp.where(inside, 1.0, 0.0))
    )
    item_scale = lax.rsqrt(item_degree.astype(jnp.float32))
    panels = (hits * item_scale[None, :]).reshape(queries, item_blocks, width)
    picked = jnp.take(panels, block_cols, axis=1)
    partial_value = jnp.einsum("qtk,tjk->qtj", picked, values_now, precision=highest)
    row_onehot = (block_rows[:, None] == jnp.arange(user_blocks, dtype=jnp.int32)[None, :]).astype(
        jnp.float32
    ) * alive_mask[:, None]
    user_terms = jnp.einsum("qtj,tu->quj", partial_value, row_onehot, precision=highest)
    user_scale = (1.0 / user_degree.astype(jnp.float32)).reshape(user_blocks, width)
    user_totals = lax.psum(user_terms, "items")
    weighted = user_totals * user_scale[None, :, :]
    picked_users = jnp.take(weighted, block_rows, axis=1)
    score_part = jnp.einsum("qtj,tjk->qtk", picked_users, values_now, precision=highest)
    block_range = jnp.arange(item_blocks, dtype=jnp.int32)
    col_onehot = (block_cols[:, None] == block_range[None, :]).astype(jnp.float32) * alive_mask[
        :, None
    ]
    score_terms = jnp.einsum("qtk,tb->qbk", score_part, col_onehot, precision=highest).reshape(
        queries, items_local
    )
    score_totals = lax.psum(score_terms, "users")
    count = queries // lax.axis_size("users")
    score_rows = lax.dynamic_slice_in_dim(score_totals, lax.axis_index("users") * count, count, 0)
    return score_rows * item_scale[None, :]


def solution(mesh):
    in_specs = (
        P(),
        P("items"),
        P("users"),
        P("users", "items", None, None, None),
        P("users", "items", None),
        P("users", "items", None),
        P("users", "items"),
    )
    out_specs = P("users", "items")
    return jax.shard_map(body, mesh=mesh, in_specs=in_specs, out_specs=out_specs, check_vma=False)
```

profile of v0, /device:TPU:30, one launch (start us, length us, event | category | flops | bytes accessed | tf_op | source)
XLA Modules:
  0.0 588.0 jit_solution(13323144484975118217)
XLA Ops:
  6.5 0.0 copy-start
  6.5 0.0 all-reduce.3.cloned.1.call-start
  6.5 0.8 fusion.25
  7.4 0.7 select_bitcast_fusion.1
  8.1 0.7 fusion.34
  8.8 0.7 compare_and_fusion
  9.4 0.7 multiply_reduce_fusion
  10.2 0.7 and_reduce_fusion
  10.9 29.5 %scatter_custom_fusion = f32[524288]{0:T(1024)} fusion(s32[4096]{0:T(1024)S(1)} %bitcast.65, f32[4096]{0:T(1024)S(1)} %bitcast.66, f32[]{:T(128)} %constant.18.clone.1), kind=kCustom, calls=%fused_computation.13 | custom fusion | flops 4096 | bytes 2097156
  40.4 2.8 reshape.100
  43.2 0.0 copy-done.1
  43.9 3.1 copy_bitcast_fusion.1
  47.0 2.2 gather_fusion
  49.2 0.0 copy-done
  49.2 2.6 fusion.4
  51.8 0.0 copy-done.3
  51.8 1.5 convolution_bitcast_fusion
  53.3 0.0 all-reduce.3.cloned.1.call-update
  53.3 0.0 all-reduce.5.cloned.1.call-start
  53.4 0.0 copy-done.2
  53.4 0.0 copy-start.4
  53.5 345.6 %all-reduce.3.cloned.1.call-done = f32[16,64,128]{2,1,0:T(8,128)} async-done(((f32[16,64,128]{2,1,0:T(8,128)}), f32[16,64,128]{2,1,0:T(8,128)}) %all-reduce.3.cloned.1.call-update) | async-done | bytes 524304 | tf_op jit(solution)/shard_map/psum | solution.py:38
  399.1 1.1 broadcast_multiply_fusion
  400.1 0.3 copy.16
  400.5 0.6 gather_fusion.1
  401.0 1.5 fusion.7
  402.5 0.0 copy-done.4
  402.5 1.9 fusion.14
  404.5 2.5 copy.28
  407.0 0.0 all-reduce.5.cloned.1.call-update
  407.0 172.2 %all-reduce.5.cloned.1.call-done = f32[16,32768]{1,0:T(8,128)} async-done(((f32[16,32768]{1,0:T(8,128)}), f32[16,32768]{1,0:T(8,128)}) %all-reduce.5.cloned.1.call-update) | async-done | bytes 2097168 | tf_op jit(solution)/shard_map/psum | solution.py:49
  579.2 2.0 dynamic-slice_multiply_fusion
  (14 shorter events, 0.1 us)
Async XLA Ops:
  6.5 42.7 %copy-start = (f32[1,1,24,128,128]{4,3,2,1,0:T(8,128)S(1)}, f32[1,1,24,128,128]{4,3,2,1,0:T(8,128)}, u32[]{:S(2)}) copy-start(f32[1,1,24,128,128]{4,3,2,1,0:T(8,128)} %param.10) | copy-start | bytes 4718596
  6.5 392.5 %all-reduce.3.cloned.1.call-start = ((), (), s32[]{:S(2)}) async-start(), calls=%async_computation | async-start | bytes 1048576 | tf_op jit(solution)/shard_map/psum | solution.py:38
  40.4 2.8 copy-start.1
  47.0 4.8 copy-start.3
  47.0 6.4 %copy-start.2 = (s32[8192]{0:T(1024)S(1)}, s32[8192]{0:T(1024)}, u32[]{:S(2)}) copy-start(s32[8192]{0:T(1024)} %param.9) | copy-start | bytes 98308
  53.3 525.9 %all-reduce.5.cloned.1.call-start = ((), (), s32[]{:S(2)}) async-start(), calls=%async_computation.1 | async-start | bytes 4194304 | tf_op jit(solution)/shard_map/psum | solution.py:49
  53.4 349.1 %copy-start.4 = (s32[1,1,24]{2,1,0:T(1,128)S(1)}, s32[1,1,24]{2,1,0:T(1,128)}, u32[]{:S(2)}) copy-start(s32[1,1,24]{2,1,0:T(1,128)} %param.12) | copy-start | bytes 292
Sparse Core Ops, SparseCore 0:
  53.4 345.5 all-reduce.2
  407.1 172.0 all-reduce.4
where the time goes:
time: 589 us; the launch traced here: 588 us
  waiting for transfers between devices  518 us (88%)
  other arithmetic  40.1 us (7%)
  between operations  14.2 us (2%)
  local copies, waits for them, and re-layouts  8.42 us (1%)
  matrix products  7.49 us (1%)
    psum x1, waiting for transfers between devices, body(): user_totals = lax.psum(user_terms, 'items')  346 us
    psum x1, waiting for transfers between devices, body(): score_totals = lax.psum(score_terms, 'users')  172 us
    unnamed x5, other arithmetic  31.7 us
  transfers between devices with their start and end apart: 2, of which 2 were waited for; matrix products, arithmetic and copies ran while one was open for 0% of the time, Pallas kernels for 0%

commit v1 on v0

v1 whole, which is shorter than its diff:
```python
import functools

import jax
import jax.numpy as jnp
from jax import lax
from jax.experimental import pallas as pl
from jax.experimental.pallas import tpu as pltpu
from jax.sharding import PartitionSpec as P

MESH = pl.DeviceIdType.MESH
F32 = jnp.float32
BF16 = jnp.bfloat16
I32 = jnp.int32
NT = (((1,), (1,)), ((), ()))
NN = (((1,), (0,)), ((), ()))


def halves(x):
    high = x.astype(BF16)
    return high, (x - high.astype(F32)).astype(BF16)


def dot(a, b, dims=NN):
    return lax.dot_general(a, b, dims, preferred_element_type=F32)


def kernel(
    slots, queries, user_blocks, item_blocks, width,
    hist, ideg, udeg, vals_any, rows, cols, count,
    out,
    vals, vhi, vlo, hits, msg1, recv1, xsend, xrecv, msg2, recv2, msg3, recv3,
    meta_r_out, meta_r, meta_c_out, meta_c, pick_r, pick_rt, pick_c, sem,
):
    n = queries
    span = slots * n
    items = lax.axis_index("items")
    user = lax.axis_index("users")
    chip, core = items // 2, lax.rem(items, 2)
    partner = {"items": chip * 2 + (1 - core)}

    def chip_peer(i):
        c = lax.rem(chip + 1 + i, n)
        return c, {"items": c * 2 + core}

    def user_peer(i):
        u = lax.rem(user + 1 + i, n)
        return u, {"users": u}

    def part(ref, i, size=slots):
        return ref.at[pl.ds(pl.multiple_of(i * size, 8), size)]

    def wait(ref, count_rows, k):
        piece = ref.at[pl.ds(0, count_rows)]
        pltpu.make_async_copy(piece, piece, sem.at[k]).wait()

    barrier = pltpu.get_barrier_semaphore()
    load = pltpu.make_async_copy(vals_any, vals, sem.at[0])
    load.start()

    @pl.loop(0, n - 1)
    def _(i):
        pl.semaphore_signal(barrier, inc=1, device_id=chip_peer(i)[1], device_id_type=MESH)
        pl.semaphore_signal(barrier, inc=1, device_id=user_peer(i)[1], device_id_type=MESH)

    pl.semaphore_signal(barrier, inc=1, device_id=partner, device_id_type=MESH)

    place = lax.broadcasted_iota(I32, (8, width), 0) * width + lax.broadcasted_iota(I32, (8, width), 1)
    sub = lax.broadcasted_iota(I32, (slots, width), 0)
    mrow = jnp.zeros((8, width), I32)
    mcol = jnp.zeros((8, width), I32)
    colv = jnp.zeros((slots, width), I32)
    alive = count[0, 0]
    for t in range(slots):
        r, c = rows[0, 0, t], cols[0, 0, t]
        live = t < alive
        mrow = jnp.where(place == chip * slots + t, jnp.where(live, r, -1), mrow)
        mcol = jnp.where(place == user * slots + t, jnp.where(live, c, -1), mcol)
        colv = jnp.where(sub == t, c, colv)
    meta_r_out[...] = mrow
    meta_c_out[...] = mcol
    part(meta_r, chip, 8)[...] = mrow
    part(meta_c, user, 8)[...] = mcol

    hlen = hist.shape[1]
    bits = width.bit_length() - 1
    colw = jnp.concatenate([colv] * (hlen // width), axis=1) + items * item_blocks
    lane_id = lax.broadcasted_iota(I32, (width, hlen), 0)
    for q in range(n):
        h = hist[q : q + 1, :]
        block = lax.shift_right_logical(h, bits) == colw
        spot = (h & (width - 1)) == lane_id
        hits[pl.ds(q, slots, stride=n), :] = dot(
            jnp.where(block, 1.0, 0.0).astype(BF16), jnp.where(spot, 1.0, 0.0).astype(BF16), NT
        )

    pl.semaphore_wait(barrier, 2 * (n - 1) + 1)

    @pl.loop(0, n - 1)
    def _(i):
        pltpu.make_async_remote_copy(
            meta_r_out, part(meta_r, chip, 8), sem.at[1], sem.at[2],
            device_id=chip_peer(i)[1], device_id_type=MESH,
        ).start()
        pltpu.make_async_remote_copy(
            meta_c_out, part(meta_c, user, 8), sem.at[3], sem.at[4],
            device_id=user_peer(i)[1], device_id_type=MESH,
        ).start()

    load.wait()

    for t in range(slots):
        degree = ideg[pl.ds(cols[0, 0, t], 1), :]
        high, low = halves(vals[t] * lax.rsqrt(degree.astype(F32)))
        vhi[t] = high
        vlo[t] = low
        h = hits[pl.ds(t * n, n), :].astype(BF16)
        msg1[pl.ds(t, n, stride=slots), :] = dot(h, high, NT) + dot(h, low, NT)

    def exchange(msg, recv, mine, peer, send_k, recv_k):
        @pl.loop(0, n - 1)
        def _(i):
            p, where = peer(i)
            pltpu.make_async_remote_copy(
                part(msg, p), part(recv, mine), sem.at[send_k], sem.at[recv_k],
                device_id=where, device_id_type=MESH,
            ).start()

        part(recv, mine)[...] = part(msg, mine)[...]

    exchange(msg1, recv1, chip, chip_peer, 5, 6)

    wait(meta_r, 8 * (n - 1), 2)
    wait(meta_c, 8 * (n - 1), 4)

    def gathered(ref):
        total = ref[0:8, :]
        for i in range(1, n):
            total = total + ref[8 * i : 8 * i + 8, :]
        return total

    ids_r, ids_c = gathered(meta_r), gathered(meta_c)
    block_r = lax.broadcasted_iota(I32, (width, width), 0)
    block_c = lax.broadcasted_iota(I32, (item_blocks, width), 0)
    for k in range(span // width):
        at = slice(k * width, (k + 1) * width)
        hot = jnp.where(ids_r[k : k + 1, :] == block_r, 1.0, 0.0)
        pick_r[:, at] = hot[:user_blocks].astype(BF16)
        pick_rt[at, :] = hot.T.astype(BF16)
        pick_c[:, at] = jnp.where(ids_c[k : k + 1, :] == block_c, 1.0, 0.0).astype(BF16)

    wait(recv1, slots * (n - 1), 6)
    high, low = halves(recv1[...])
    acc = dot(pick_r[...], high) + dot(pick_r[...], low)
    xsend[...] = acc
    cross = pltpu.make_async_remote_copy(
        xsend, xrecv, sem.at[7], sem.at[8], device_id=partner, device_id_type=MESH
    )
    cross.start()
    cross.wait()
    weights = (acc + xrecv[...]) / udeg[...].astype(F32)
    high, low = halves(weights)
    back = pick_rt[:, :user_blocks]
    msg2[...] = dot(back, high) + dot(back, low)
    exchange(msg2, recv2, chip, chip_peer, 9, 10)
    wait(recv2, slots * (n - 1), 10)

    for t in range(slots):
        high, low = halves(recv2[pl.ds(t, n, stride=slots), :])
        msg3[pl.ds(t, n, stride=slots), :] = dot(high, vhi[t]) + dot(low, vhi[t]) + dot(high, vlo[t])

    exchange(msg3, recv3, user, user_peer, 11, 12)
    wait(recv3, slots * (n - 1), 12)
    high, low = halves(recv3[...])
    out[...] = dot(pick_c[...], high) + dot(pick_c[...], low)

    wait(meta_r, 8 * (n - 1), 1)
    wait(meta_c, 8 * (n - 1), 3)
    wait(msg1, slots * (n - 1), 5)
    wait(msg2, slots * (n - 1), 9)
    wait(msg3, slots * (n - 1), 11)


def body(histories, item_degree, user_degree, tile_values, tile_rows, tile_cols, tile_count):
    queries = histories.shape[0]
    slots, width = tile_values.shape[2], tile_values.shape[-1]
    item_blocks = item_degree.shape[0] // width
    user_blocks = user_degree.shape[0] // width
    span = slots * queries
    vmem = pl.BlockSpec(memory_space=pltpu.VMEM)
    smem = pl.BlockSpec(memory_space=pltpu.SMEM)
    panel = pltpu.VMEM((span, width), F32)
    scores = pl.pallas_call(
        functools.partial(kernel, slots, queries, user_blocks, item_blocks, width),
        out_shape=jax.ShapeDtypeStruct((item_blocks, width), F32),
        in_specs=[vmem, vmem, vmem, pl.BlockSpec(memory_space=pl.ANY), smem, smem, smem],
        out_specs=vmem,
        scratch_shapes=[
            pltpu.VMEM((slots, width, width), F32),
            pltpu.VMEM((slots, width, width), BF16),
            pltpu.VMEM((slots, width, width), BF16),
            panel, panel, panel,
            pltpu.VMEM((user_blocks, width), F32),
            pltpu.VMEM((user_blocks, width), F32),
            panel, panel, panel, panel,
            pltpu.VMEM((8, width), I32),
            pltpu.VMEM((8 * queries, width), I32),
            pltpu.VMEM((8, width), I32),
            pltpu.VMEM((8 * queries, width), I32),
            pltpu.VMEM((user_blocks, span), BF16),
            pltpu.VMEM((span, width), BF16),
            pltpu.VMEM((item_blocks, span), BF16),
            pltpu.SemaphoreType.DMA((13,)),
        ],
        compiler_params=pltpu.CompilerParams(
            collective_id=0, has_side_effects=True, vmem_limit_bytes=32 * 1024 * 1024
        ),
        cost_estimate=pl.CostEstimate(flops=10**8, bytes_accessed=4 * 10**6, transcendentals=0),
    )(
        histories,
        item_degree.reshape(item_blocks, width),
        user_degree.reshape(user_blocks, width),
        tile_values.reshape(slots, width, width),
        tile_rows, tile_cols, tile_count,
    )
    return scores.reshape(1, item_blocks * width)


def solution(mesh):
    in_specs = (
        P(),
        P("items"),
        P("users"),
        P("users", "items", None, None, None),
        P("users", "items", None),
        P("users", "items", None),
        P("users", "items"),
    )
    out_specs = P("users", "items")
    return jax.shard_map(body, mesh=mesh, in_specs=in_specs, out_specs=out_specs, check_vma=False)
```

time: 589 us -> 53.5 us (0.09)
  the two profiles are of different devices: /device:TPU:30 before, /device:TPU:1 now
where the time goes in v1:
time: 53.5 us; the launch traced here: 53.1 us
  Pallas kernels  46.7 us (87%)
  local copies, waits for them, and re-layouts  5.75 us (11%)
  between operations  0.67 us (1%)
    pallas_call x1, Pallas kernels, body(): pl.pallas_call(functools.partial(kernel, slots, queries, user_blocks, ite...  46.7 us
    unnamed x13, local copies, waits for them, and re-layouts  5.75 us

profile of v1, /device:TPU:1, one launch (start us, length us, event | category | flops | bytes accessed | tf_op | source)
XLA Modules:
  0.0 53.1 jit_solution(1753613201050005033)
XLA Ops:
  0.7 0.0 copy-start
  0.7 1.4 %copy-done = f32[1,1,24,128,128]{4,3,2,1,0:T(8,128)S(1)} copy-done((f32[1,1,24,128,128]{4,3,2,1,0:T(8,128)S(1)}, f32[1,1,24,128,128]{4,3,2,1,0:T(8,128)}, u32[]{:S(2)}) %copy-start) | copy-done | bytes 1572888
  2.1 0.0 copy-start.1
  2.1 0.9 %copy-done.1 = s32[32768]{0:T(1024)S(1)} copy-done((s32[32768]{0:T(1024)S(1)}, s32[32768]{0:T(1024)}, u32[]{:S(2)}) %copy-start.1) | copy-done | bytes 131096
  3.0 0.0 copy-start.2
  3.0 0.8 %copy-done.2 = s32[8192]{0:T(1024)S(1)} copy-done((s32[8192]{0:T(1024)S(1)}, s32[8192]{0:T(1024)}, u32[]{:S(2)}) %copy-start.2) | copy-done | bytes 32792
  3.7 0.0 copy-start.3
  3.7 0.7 %copy-done.3 = s32[16,256]{1,0:T(8,128)S(1)} copy-done((s32[16,256]{1,0:T(8,128)S(1)}, s32[16,256]{1,0:T(8,128)}, u32[]{:S(2)}) %copy-start.3) | copy-done | bytes 16408
  4.4 0.0 copy-start.4
  4.4 0.7 %copy-done.4 = s32[1,1,24]{2,1,0:T(1,128)S(1)} copy-done((s32[1,1,24]{2,1,0:T(1,128)S(1)}, s32[1,1,24]{2,1,0:T(1,128)}, u32[]{:S(2)}) %copy-start.4) | copy-done | bytes 120
  5.1 0.0 copy-start.5
  5.1 0.7 %copy-done.5 = s32[1,1,24]{2,1,0:T(1,128)S(1)} copy-done((s32[1,1,24]{2,1,0:T(1,128)S(1)}, s32[1,1,24]{2,1,0:T(1,128)}, u32[]{:S(2)}) %copy-start.5) | copy-done | bytes 120
  5.8 46.7 %shard_map.73 = f32[256,128]{1,0:T(8,128)S(1)} custom-call(s32[16,256]{1,0:T(8,128)S(1)} %copy-done.3, s32[256,128]{1,0:T(8,128)S(1)} %bitcast.6, s32[64,128]{1,0:T(8,128)S(1)} %bitcast.7, f32[24,128,128]{2,1,0:T(8,128)S(1)} %bitcast.4, s32[1,1,24]{2,1,0:T(1,128)S(1)} %copy-done.4, s32[1,1,24]{2,1,0:T(1,128)S(1)} %copy-done.5, s32[1,1]{1,0:T(1,128)S(6)} %copy.9.count), custom_call_target="tpu_custom_call" | custom-call | flops 100000000 | bytes 4000000 | tf_op jit(solution)/shard_map/pallas_call | solution.py:192
  52.5 0.7 %copy.10 = f32[1,32768]{1,0:T(1,128)} copy(f32[1,32768]{1,0:T(1,128)S(1)} %bitcast.5) | data formatting | bytes 262144
Async XLA Ops:
  0.7 1.4 %copy-start = (f32[1,1,24,128,128]{4,3,2,1,0:T(8,128)S(1)}, f32[1,1,24,128,128]{4,3,2,1,0:T(8,128)}, u32[]{:S(2)}) copy-start(f32[1,1,24,128,128]{4,3,2,1,0:T(8,128)} %param.10) | copy-start | bytes 4718596
  2.1 0.9 %copy-start.1 = (s32[32768]{0:T(1024)S(1)}, s32[32768]{0:T(1024)}, u32[]{:S(2)}) copy-start(s32[32768]{0:T(1024)} %param.8) | copy-start | bytes 393220
  3.0 0.8 %copy-start.2 = (s32[8192]{0:T(1024)S(1)}, s32[8192]{0:T(1024)}, u32[]{:S(2)}) copy-start(s32[8192]{0:T(1024)} %param.9) | copy-start | bytes 98308
  3.7 0.7 %copy-start.3 = (s32[16,256]{1,0:T(8,128)S(1)}, s32[16,256]{1,0:T(8,128)}, u32[]{:S(2)}) copy-start(s32[16,256]{1,0:T(8,128)} %hist.1) | copy-start | bytes 49156
  4.4 0.7 %copy-start.4 = (s32[1,1,24]{2,1,0:T(1,128)S(1)}, s32[1,1,24]{2,1,0:T(1,128)}, u32[]{:S(2)}) copy-start(s32[1,1,24]{2,1,0:T(1,128)} %rows.1) | copy-start | bytes 292
  5.1 0.7 %copy-start.5 = (s32[1,1,24]{2,1,0:T(1,128)S(1)}, s32[1,1,24]{2,1,0:T(1,128)}, u32[]{:S(2)}) copy-start(s32[1,1,24]{2,1,0:T(1,128)} %cols.1) | copy-start | bytes 292

commit v2 on v1

v2 whole, which is shorter than its diff:
```python
import functools

import jax
import jax.numpy as jnp
from jax import lax
from jax.experimental import pallas as pl
from jax.experimental.pallas import tpu as pltpu
from jax.sharding import PartitionSpec as P

MESH = pl.DeviceIdType.MESH
F32 = jnp.float32
BF16 = jnp.bfloat16
I32 = jnp.int32
NT = (((1,), (1,)), ((), ()))
NN = (((1,), (0,)), ((), ()))


def halves(x):
    high = x.astype(BF16)
    return high, (x - high.astype(F32)).astype(BF16)


def dot(a, b, dims=NN):
    return lax.dot_general(a, b, dims, preferred_element_type=F32)


GROUPS = 4


def kernel(slots, queries, user_blocks, item_blocks, width, *refs):
    inputs, out, local = refs[:7], refs[7], refs[8:15]
    (
        vhi, vlo, hits, msg1, recv1, xsend, xrecv, msg2, recv2, msg3, recv3,
        meta_r_out, meta_r, meta_c_out, meta_c, pick_r, pick_rt, pick_c,
        load_sem, back_sem, sem,
    ) = refs[15:]
    hist, ideg, udeg, vals, rows, cols, count = local
    n = queries
    span = slots * n
    items = lax.axis_index("items")
    user = lax.axis_index("users")
    z, y_hi, core = items // 4, lax.rem(items // 2, 2), lax.rem(items, 2)
    run = n // 4
    chip = ((z // run) * 2 + y_hi) * run + lax.rem(z, run)
    partner = {"items": items + 1 - 2 * core}
    per = n // GROUPS

    def at_chip(c):
        z = (c // (2 * run)) * run + lax.rem(c, run)
        return {"items": (z * 2 + lax.rem(c // run, 2)) * 2 + core}

    def others(me, start, stop, action, backwards=False):
        @pl.loop(start, stop)
        def _(i):
            p = start + stop - 1 - i if backwards else i

            @pl.when(p != me)
            def _():
                action(p)

    def send(src, dst, send_k, recv_sem, where):
        pltpu.make_async_remote_copy(
            src, dst, sem.at[send_k], recv_sem, device_id=where, device_id_type=MESH
        ).start()

    def part(ref, i, size=slots):
        return ref.at[pl.ds(pl.multiple_of(i * size, 8), size)]

    def wait(ref, count_rows, k):
        piece = ref.at[pl.ds(0, count_rows)]
        pltpu.make_async_copy(piece, piece, sem.at[k]).wait()

    barrier = pltpu.get_barrier_semaphore()
    loads = [pltpu.make_async_copy(inputs[i], local[i], load_sem.at[i]) for i in range(7)]
    for i in (4, 5, 6, 0, 1, 3, 2):
        loads[i].start()

    def greet(where):
        pl.semaphore_signal(barrier, inc=1, device_id=where, device_id_type=MESH)

    others(chip, 0, n, lambda p: greet(at_chip(p)))
    others(user, 0, n, lambda p: greet({"users": p}))
    greet(partner)

    place = lax.broadcasted_iota(I32, (8, width), 0) * width + lax.broadcasted_iota(I32, (8, width), 1)
    sub = lax.broadcasted_iota(I32, (slots, width), 0)
    for i in (4, 5, 6):
        loads[i].wait()
    mrow = jnp.zeros((8, width), I32)
    mcol = jnp.zeros((8, width), I32)
    colv = jnp.zeros((slots, width), I32)
    alive = count[0, 0]
    for t in range(slots):
        r, c = rows[0, 0, t], cols[0, 0, t]
        live = t < alive
        mrow = jnp.where(place == chip * slots + t, jnp.where(live, r, -1), mrow)
        mcol = jnp.where(place == user * slots + t, jnp.where(live, c, -1), mcol)
        colv = jnp.where(sub == t, c, colv)
    meta_r_out[...] = mrow
    meta_c_out[...] = mcol
    part(meta_r, chip, 8)[...] = mrow
    part(meta_c, user, 8)[...] = mcol

    loads[0].wait()
    hlen = hist.shape[1]
    bits = width.bit_length() - 1
    colw = jnp.concatenate([colv] * (hlen // width), axis=1) + items * item_blocks
    lane_id = lax.broadcasted_iota(I32, (width, hlen), 0)
    for q in range(n):
        h = hist[q : q + 1, :]
        block = lax.shift_right_logical(h, bits) == colw
        spot = (h & (width - 1)) == lane_id
        hits[pl.ds(q, slots, stride=n), :] = dot(
            jnp.where(block, 1.0, 0.0).astype(BF16), jnp.where(spot, 1.0, 0.0).astype(BF16), NT
        )

    loads[1].wait()
    loads[3].wait()

    for t in range(slots):
        degree = ideg[pl.ds(cols[0, 0, t], 1), :]
        high, low = halves(vals[t] * lax.rsqrt(degree.astype(F32)))
        vhi[t] = high
        vlo[t] = low
        h = hits[pl.ds(t * n, n), :].astype(BF16)
        msg1[pl.ds(t, n, stride=slots), :] = dot(h, high, NT) + dot(h, low, NT)

    pl.semaphore_wait(barrier, 2 * (n - 1) + 1)

    def forth(p):
        send(meta_r_out, part(meta_r, chip, 8), 1, sem.at[2], at_chip(p))
        send(part(msg1, p), part(recv1, chip), 5, sem.at[6], at_chip(p))

    others(chip, 0, n, forth, backwards=True)
    part(recv1, chip)[...] = part(msg1, chip)[...]
    others(user, 0, n, lambda p: send(meta_c_out, part(meta_c, user, 8), 3, sem.at[4], {"users": p}))

    def gathered(ref):
        total = ref[0:8, :]
        for i in range(1, n):
            total = total + ref[8 * i : 8 * i + 8, :]
        return total

    wait(meta_r, 8 * (n - 1), 2)
    ids = gathered(meta_r)
    block = lax.broadcasted_iota(I32, (width, width), 0)
    for k in range(span // width):
        at = slice(k * width, (k + 1) * width)
        hot = jnp.where(ids[k : k + 1, :] == block, 1.0, 0.0)
        pick_r[:, at] = hot[:user_blocks].astype(BF16)
        pick_rt[at, :] = hot.T.astype(BF16)

    wait(recv1, slots * (n - 1), 6)
    high, low = halves(recv1[...])
    acc = dot(pick_r[...], high) + dot(pick_r[...], low)
    xsend[...] = acc
    cross = pltpu.make_async_remote_copy(
        xsend, xrecv, sem.at[7], sem.at[8], device_id=partner, device_id_type=MESH
    )
    cross.start()
    cross.wait()
    loads[2].wait()
    weights = (acc + xrecv[...]) / udeg[...].astype(F32)
    high, low = halves(weights)
    back = pick_rt[:, :user_blocks]
    msg2[...] = dot(back, high) + dot(back, low)
    mine = back_sem.at[chip // per]
    others(chip, 0, n, lambda p: send(part(msg2, p), part(recv2, chip), 9, mine, at_chip(p)))
    part(recv2, chip)[...] = part(msg2, chip)[...]

    wait(meta_c, 8 * (n - 1), 4)
    ids = gathered(meta_c)
    block = lax.broadcasted_iota(I32, (item_blocks, width), 0)
    for k in range(span // width):
        at = slice(k * width, (k + 1) * width)
        pick_c[:, at] = jnp.where(ids[k : k + 1, :] == block, 1.0, 0.0).astype(BF16)

    @pl.loop(0, GROUPS)
    def _(g):
        own = chip // per == g
        for came, senders in ((own, per - 1), (jnp.logical_not(own), per)):

            @pl.when(came)
            def _():
                piece = recv2.at[pl.ds(0, slots * senders)]
                pltpu.make_async_copy(piece, piece, back_sem.at[g]).wait()

        for t in range(slots):
            spots = pl.ds(g * (per * slots) + t, per, stride=slots)
            high, low = halves(recv2[spots, :])
            msg3[spots, :] = dot(high, vhi[t]) + dot(low, vhi[t]) + dot(high, vlo[t])

        others(
            user, g * per, (g + 1) * per,
            lambda p: send(part(msg3, p), part(recv3, user), 11, sem.at[12], {"users": p}),
        )

    part(recv3, user)[...] = part(msg3, user)[...]
    wait(recv3, slots * (n - 1), 12)
    high, low = halves(recv3[...])
    out[...] = dot(pick_c[...], high) + dot(pick_c[...], low)

    wait(meta_r, 8 * (n - 1), 1)
    wait(meta_c, 8 * (n - 1), 3)
    wait(msg1, slots * (n - 1), 5)
    wait(msg2, slots * (n - 1), 9)
    wait(msg3, slots * (n - 1), 11)


def body(histories, item_degree, user_degree, tile_values, tile_rows, tile_cols, tile_count):
    queries = histories.shape[0]
    slots, width = tile_values.shape[2], tile_values.shape[-1]
    item_blocks = item_degree.shape[0] // width
    user_blocks = user_degree.shape[0] // width
    span = slots * queries
    vmem = pl.BlockSpec(memory_space=pltpu.VMEM)
    panel = pltpu.VMEM((span, width), F32)
    scores = pl.pallas_call(
        functools.partial(kernel, slots, queries, user_blocks, item_blocks, width),
        out_shape=jax.ShapeDtypeStruct((item_blocks, width), F32),
        in_specs=[pl.BlockSpec(memory_space=pltpu.HBM)] * 7,
        out_specs=vmem,
        scratch_shapes=[
            pltpu.VMEM(histories.shape, I32),
            pltpu.VMEM((item_blocks, width), I32),
            pltpu.VMEM((user_blocks, width), I32),
            pltpu.VMEM((slots, width, width), F32),
            pltpu.SMEM(tile_rows.shape, I32),
            pltpu.SMEM(tile_cols.shape, I32),
            pltpu.SMEM(tile_count.shape, I32),
            pltpu.VMEM((slots, width, width), BF16),
            pltpu.VMEM((slots, width, width), BF16),
            panel, panel, panel,
            pltpu.VMEM((user_blocks, width), F32),
            pltpu.VMEM((user_blocks, width), F32),
            panel, panel, panel, panel,
            pltpu.VMEM((8, width), I32),
            pltpu.VMEM((8 * queries, width), I32),
            pltpu.VMEM((8, width), I32),
            pltpu.VMEM((8 * queries, width), I32),
            pltpu.VMEM((user_blocks, span), BF16),
            pltpu.VMEM((span, width), BF16),
            pltpu.VMEM((item_blocks, span), BF16),
            pltpu.SemaphoreType.DMA((7,)),
            pltpu.SemaphoreType.DMA((GROUPS,)),
            pltpu.SemaphoreType.DMA((13,)),
        ],
        compiler_params=pltpu.CompilerParams(
            collective_id=0, has_side_effects=True, vmem_limit_bytes=63 * 1024 * 1024
        ),
        cost_estimate=pl.CostEstimate(flops=10**8, bytes_accessed=4 * 10**6, transcendentals=0),
    )(
        histories,
        item_degree.reshape(item_blocks, width),
        user_degree.reshape(user_blocks, width),
        tile_values.reshape(slots, width, width),
        tile_rows, tile_cols, tile_count,
    )
    return scores.reshape(1, item_blocks * width)


def solution(mesh):
    in_specs = (
        P(),
        P("items"),
        P("users"),
        P("users", "items", None, None, None),
        P("users", "items", None),
        P("users", "items", None),
        P("users", "items"),
    )
    out_specs = P("users", "items")
    return jax.shard_map(body, mesh=mesh, in_specs=in_specs, out_specs=out_specs, check_vma=False)
```

time: 53.5 us -> 45.5 us (0.85)
  the two profiles are of different devices: /device:TPU:1 before, /device:TPU:24 now
where the time goes in v2:
time: 45.5 us; the launch traced here: 45.3 us
  Pallas kernels  43.1 us (95%)
  local copies, waits for them, and re-layouts  1.57 us (3%)
  between operations  0.66 us (1%)
    pallas_call x1, Pallas kernels, body(): pl.pallas_call(functools.partial(kernel, slots, queries, user_blocks, ite...  43.1 us
    unnamed x1, local copies, waits for them, and re-layouts  1.57 us

profile of v2, /device:TPU:24, one launch (start us, length us, event | category | flops | bytes accessed | tf_op | source)
XLA Modules:
  0.0 45.3 jit_solution(12946364243171383910)
XLA Ops:
  0.7 43.1 %shard_map.73 = f32[256,128]{1,0:T(8,128)} custom-call(s32[16,256]{1,0:T(8,128)} %refs_0_.1, s32[256,128]{1,0:T(8,128)} %bitcast.6, s32[64,128]{1,0:T(8,128)} %bitcast.7, f32[24,128,128]{2,1,0:T(8,128)} %bitcast.4, s32[1,1,24]{2,1,0:T(1,128)} %refs_4_.1, s32[1,1,24]{2,1,0:T(1,128)} %refs_5_.1, s32[1,1]{1,0:T(1,128)S(6)} %copy.9.refs_6_), custom_call_target="tpu_custom_call" | custom-call | flops 100000000 | bytes 4000000 | tf_op jit(solution)/shard_map/pallas_call | solution.py:218
  43.8 1.6 %copy.10 = f32[1,32768]{1,0:T(1,128)} copy(f32[1,32768]{1,0:T(1,128)} %bitcast.5) | data formatting | bytes 262144

commit v3 on v2

--- a/solution.py
+++ b/solution.py
@@ -31,8 +31,9 @@
     inputs, out, local = refs[:7], refs[7], refs[8:15]
     (
         vhi, vlo, hits, msg1, recv1, xsend, xrecv, msg2, recv2, msg3, recv3,
+        recv1b, xsendb, xrecvb, msg2b,
         meta_r_out, meta_r, meta_c_out, meta_c, pick_r, pick_rt, pick_c,
-        load_sem, back_sem, sem,
+        load_sem, back_sem, ready, sem,
     ) = refs[15:]
     hist, ideg, udeg, vals, rows, cols, count = local
     n = queries
@@ -41,13 +42,21 @@
     user = lax.axis_index("users")
     z, y_hi, core = items // 4, lax.rem(items // 2, 2), lax.rem(items, 2)
     run = n // 4
-    chip = ((z // run) * 2 + y_hi) * run + lax.rem(z, run)
+    chip = (y_hi * 2 + z // run) * run + lax.rem(z, run)
+    owners = 3 * run
     partner = {"items": items + 1 - 2 * core}
     per = n // GROUPS
+    step = user // run
+    order = (step + y_hi * (run - 1 - 2 * step)) * run + lax.rem(user, run)
 
     def at_chip(c):
-        z = (c // (2 * run)) * run + lax.rem(c, run)
-        return {"items": (z * 2 + lax.rem(c // run, 2)) * 2 + core}
+        half = c // run
+        z = lax.rem(half, 2) * run + lax.rem(c, run)
+        return {"items": (z * 2 + half // 2) * 2 + core}
+
+    def at_order(p):
+        s = p // run
+        return {"users": (s + y_hi * (run - 1 - 2 * s)) * run + lax.rem(p, run)}
 
     def others(me, start, stop, action, backwards=False):
         @pl.loop(start, stop)
@@ -78,9 +87,15 @@
     def greet(where):
         pl.semaphore_signal(barrier, inc=1, device_id=where, device_id_type=MESH)
 
-    others(chip, 0, n, lambda p: greet(at_chip(p)))
-    others(user, 0, n, lambda p: greet({"users": p}))
+    @pl.when(chip < owners)
+    def _():
+        others(chip, 0, n, lambda p: greet(at_chip(p)))
+
     greet(partner)
+
+    @pl.loop(order + 1, n)
+    def _(p):
+        greet(at_order(p))
 
     place = lax.broadcasted_iota(I32, (8, width), 0) * width + lax.broadcasted_iota(I32, (8, width), 1)
     sub = lax.broadcasted_iota(I32, (slots, width), 0)
@@ -125,15 +140,42 @@
         h = hits[pl.ds(t * n, n), :].astype(BF16)
         msg1[pl.ds(t, n, stride=slots), :] = dot(h, high, NT) + dot(h, low, NT)
 
-    pl.semaphore_wait(barrier, 2 * (n - 1) + 1)
-
-    def forth(p):
-        send(meta_r_out, part(meta_r, chip, 8), 1, sem.at[2], at_chip(p))
-        send(part(msg1, p), part(recv1, chip), 5, sem.at[6], at_chip(p))
-
-    others(chip, 0, n, forth, backwards=True)
-    part(recv1, chip)[...] = part(msg1, chip)[...]
-    others(user, 0, n, lambda p: send(meta_c_out, part(meta_c, user, 8), 3, sem.at[4], {"users": p}))
+    pl.semaphore_wait(barrier, owners - (chip < owners).astype(I32) + order + 1)
+
+    def forth(first, shift, recv, recv_k):
+        def action(q):
+            send(part(msg1, q), part(recv, chip), 5, sem.at[recv_k], at_chip(q - shift))
+
+        others(chip + shift, first, first + run, action)
+
+    others(chip, 0, owners, lambda p: send(meta_r_out, part(meta_r, chip, 8), 1, sem.at[2], at_chip(p)), True)
+    forth(3 * run, run, recv1, 6)
+    forth(0, 0, recv1, 6)
+    forth(2 * run, 2 * run, recv1b, 13)
+    forth(run, 0, recv1, 6)
+
+    @pl.loop(0, order)
+    def _(p):
+        pl.semaphore_signal(ready, inc=1, device_id=at_order(p), device_id_type=MESH)
+
+    def total(recv, recv_k, q, out_ref, in_ref, cross_k, msg, back_k):
+        part(recv, chip)[...] = part(msg1, q)[...]
+        wait(recv, slots * (n - 1), recv_k)
+        high, low = halves(recv[...])
+        acc = dot(pick_r[...], high) + dot(pick_r[...], low)
+        out_ref[...] = acc
+        cross = pltpu.make_async_remote_copy(
+            out_ref, in_ref, sem.at[cross_k], sem.at[cross_k + 1], device_id=partner, device_id_type=MESH
+        )
+        cross.start()
+        cross.wait()
+        weights = (acc + in_ref[...]) / udeg[...].astype(F32)
+        high, low = halves(weights)
+        back = pick_rt[:, :user_blocks]
+        msg[...] = dot(back, high) + dot(back, low)
+        mine = back_sem.at[q // per]
+        others(chip, 0, n, lambda p: send(part(msg, p), part(recv2, q), back_k, mine, at_chip(p)))
+        part(recv2, q)[...] = part(msg, chip)[...]
 
     def gathered(ref):
         total = ref[0:8, :]
@@ -141,70 +183,82 @@
             total = total + ref[8 * i : 8 * i + 8, :]
         return total
 
-    wait(meta_r, 8 * (n - 1), 2)
-    ids = gathered(meta_r)
-    block = lax.broadcasted_iota(I32, (width, width), 0)
-    for k in range(span // width):
-        at = slice(k * width, (k + 1) * width)
-        hot = jnp.where(ids[k : k + 1, :] == block, 1.0, 0.0)
-        pick_r[:, at] = hot[:user_blocks].astype(BF16)
-        pick_rt[at, :] = hot.T.astype(BF16)
-
-    wait(recv1, slots * (n - 1), 6)
-    high, low = halves(recv1[...])
-    acc = dot(pick_r[...], high) + dot(pick_r[...], low)
-    xsend[...] = acc
-    cross = pltpu.make_async_remote_copy(
-        xsend, xrecv, sem.at[7], sem.at[8], device_id=partner, device_id_type=MESH
-    )
-    cross.start()
-    cross.wait()
     loads[2].wait()
-    weights = (acc + xrecv[...]) / udeg[...].astype(F32)
-    high, low = halves(weights)
-    back = pick_rt[:, :user_blocks]
-    msg2[...] = dot(back, high) + dot(back, low)
-    mine = back_sem.at[chip // per]
-    others(chip, 0, n, lambda p: send(part(msg2, p), part(recv2, chip), 9, mine, at_chip(p)))
-    part(recv2, chip)[...] = part(msg2, chip)[...]
-
+
+    @pl.when(chip < owners)
+    def _():
+        wait(meta_r, 8 * (n - 1), 2)
+        ids = gathered(meta_r)
+        block = lax.broadcasted_iota(I32, (width, width), 0)
+        for k in range(span // width):
+            at = slice(k * width, (k + 1) * width)
+            hot = jnp.where(ids[k : k + 1, :] == block, 1.0, 0.0)
+            pick_r[:, at] = hot[:user_blocks].astype(BF16)
+            pick_rt[at, :] = hot.T.astype(BF16)
+        first = chip + (chip // (2 * run)) * run
+        total(recv1, 6, first, xsend, xrecv, 7, msg2, 9)
+
+    @pl.when(chip < run)
+    def _():
+        total(recv1b, 13, chip + 2 * run, xsendb, xrecvb, 14, msg2b, 10)
+
+    @pl.when(order < n - 1)
+    def _():
+        pl.semaphore_wait(ready, n - 1 - order)
+
+    others(user, 0, n, lambda p: send(meta_c_out, part(meta_c, user, 8), 3, sem.at[4], {"users": p}))
+
+    @pl.loop(0, GROUPS)
+    def _(g):
+        own = chip // per == jnp.where(g < 2, g, 2 * g - 4)
+        for came, senders in ((own, per - 1), (jnp.logical_not(own), per)):
+
+            @pl.when(came)
+            def _():
+                piece = recv2.at[pl.ds(0, slots * senders)]
+                pltpu.make_async_copy(piece, piece, back_sem.at[g]).wait()
+
+        for t in range(slots):
+            spots = pl.ds(g * (per * slots) + t, per, stride=slots)
+            high, low = halves(recv2[spots, :])
+            msg3[spots, :] = dot(high, vhi[t]) + dot(low, vhi[t]) + dot(high, vlo[t])
+
+        others(
+            user, g * per, (g + 1) * per,
+            lambda p: send(part(msg3, p), part(recv3, user), 11, sem.at[12], {"users": p}),
+        )
+
+    part(recv3, user)[...] = part(msg3, user)[...]
     wait(meta_c, 8 * (n - 1), 4)
     ids = gathered(meta_c)
     block = lax.broadcasted_iota(I32, (item_blocks, width), 0)
     for k in range(span // width):
         at = slice(k * width, (k + 1) * width)
         pick_c[:, at] = jnp.where(ids[k : k + 1, :] == block, 1.0, 0.0).astype(BF16)
-
-    @pl.loop(0, GROUPS)
-    def _(g):
-        own = chip // per == g
-        for came, senders in ((own, per - 1), (jnp.logical_not(own), per)):
-
-            @pl.when(came)
-            def _():
-                piece = recv2.at[pl.ds(0, slots * senders)]
-                pltpu.make_async_copy(piece, piece, back_sem.at[g]).wait()
-
-        for t in range(slots):
-            spots = pl.ds(g * (per * slots) + t, per, stride=slots)
-            high, low = halves(recv2[spots, :])
-            msg3[spots, :] = dot(high, vhi[t]) + dot(low, vhi[t]) + dot(high, vlo[t])
-
-        others(
-            user, g * per, (g + 1) * per,
-            lambda p: send(part(msg3, p), part(recv3, user), 11, sem.at[12], {"users": p}),
-        )
-
-    part(recv3, user)[...] = part(msg3, user)[...]
     wait(recv3, slots * (n - 1), 12)
     high, low = halves(recv3[...])
     out[...] = dot(pick_c[...], high) + dot(pick_c[...], low)
 
-    wait(meta_r, 8 * (n - 1), 1)
     wait(meta_c, 8 * (n - 1), 3)
-    wait(msg1, slots * (n - 1), 5)
-    wait(msg2, slots * (n - 1), 9)
     wait(msg3, slots * (n - 1), 11)
+    for here, queries_sent, ids_sent in (
+        (chip < run, n - 2, owners - 1),
+        ((chip >= run) & (chip < owners), n - 1, owners - 1),
+        (chip >= owners, n, owners),
+    ):
+
+        @pl.when(here)
+        def _():
+            wait(meta_r, 8 * ids_sent, 1)
+            wait(msg1, slots * queries_sent, 5)
+
+    @pl.when(chip < owners)
+    def _():
+        wait(msg2, slots * (n - 1), 9)
+
+    @pl.when(chip < run)
+    def _():
+        wait(msg2b, slots * (n - 1), 10)
 
 
 def body(histories, item_degree, user_degree, tile_values, tile_rows, tile_cols, tile_count):
@@ -234,6 +288,10 @@
             pltpu.VMEM((user_blocks, width), F32),
             pltpu.VMEM((user_blocks, width), F32),
             panel, panel, panel, panel,
+            panel,
+            pltpu.VMEM((user_blocks, width), F32),
+            pltpu.VMEM((user_blocks, width), F32),
+            panel,
             pltpu.VMEM((8, width), I32),
             pltpu.VMEM((8 * queries, width), I32),
             pltpu.VMEM((8, width), I32),
@@ -243,7 +301,8 @@
             pltpu.VMEM((item_blocks, span), BF16),
             pltpu.SemaphoreType.DMA((7,)),
             pltpu.SemaphoreType.DMA((GROUPS,)),
-            pltpu.SemaphoreType.DMA((13,)),
+            pltpu.SemaphoreType.REGULAR,
+            pltpu.SemaphoreType.DMA((16,)),
         ],
         compiler_params=pltpu.CompilerParams(
             collective_id=0, has_side_effects=True, vmem_limit_bytes=63 * 1024 * 1024

time: 45.5 us -> 49.3 us (1.084)
  the two profiles are of different devices: /device:TPU:24 before, /device:TPU:56 now
where the time goes in v3:
time: 49.3 us; the launch traced here: 49.1 us
  Pallas kernels  46.9 us (95%)
  local copies, waits for them, and re-layouts  1.57 us (3%)
  between operations  0.66 us (1%)
    pallas_call x1, Pallas kernels, body(): pl.pallas_call(functools.partial(kernel, slots, queries, user_blocks, ite...  46.9 us
    unnamed x1, local copies, waits for them, and re-layouts  1.57 us

profile of v3, /device:TPU:56, one launch (start us, length us, event | category | flops | bytes accessed | tf_op | source)
XLA Modules:
  0.0 49.1 jit_solution(15994127579026546286)
XLA Ops:
  0.7 46.9 %shard_map.73 = f32[256,128]{1,0:T(8,128)} custom-call(s32[16,256]{1,0:T(8,128)} %refs_0_.1, s32[256,128]{1,0:T(8,128)} %bitcast.6, s32[64,128]{1,0:T(8,128)} %bitcast.7, f32[24,128,128]{2,1,0:T(8,128)} %bitcast.4, s32[1,1,24]{2,1,0:T(1,128)} %refs_4_.1, s32[1,1,24]{2,1,0:T(1,128)} %refs_5_.1, s32[1,1]{1,0:T(1,128)S(6)} %copy.9.refs_6_), custom_call_target="tpu_custom_call" | custom-call | flops 100000000 | bytes 4000000 | tf_op jit(solution)/shard_map/pallas_call | solution.py:272
  47.6 1.6 %copy.10 = f32[1,32768]{1,0:T(1,128)} copy(f32[1,32768]{1,0:T(1,128)} %bitcast.5) | data formatting | bytes 262144

commit v4 on v2

--- a/solution.py
+++ b/solution.py
@@ -24,7 +24,7 @@
     return lax.dot_general(a, b, dims, preferred_element_type=F32)
 
 
-GROUPS = 4
+OWNED = (0, 1, 4, 3, 8, 9, 11, 12, 2, 5, 7, 6, 13, 10, 15, 14)
 
 
 def kernel(slots, queries, user_blocks, item_blocks, width, *refs):
@@ -40,23 +40,28 @@
     items = lax.axis_index("items")
     user = lax.axis_index("users")
     z, y_hi, core = items // 4, lax.rem(items // 2, 2), lax.rem(items, 2)
-    run = n // 4
-    chip = ((z // run) * 2 + y_hi) * run + lax.rem(z, run)
+    depth, run = n // 2, n // 4
     partner = {"items": items + 1 - 2 * core}
-    per = n // GROUPS
-
-    def at_chip(c):
-        z = (c // (2 * run)) * run + lax.rem(c, run)
-        return {"items": (z * 2 + lax.rem(c // run, 2)) * 2 + core}
-
-    def others(me, start, stop, action, backwards=False):
-        @pl.loop(start, stop)
+
+    def chip_of(z, y):
+        return ((z // run) * 2 + y) * run + lax.rem(z, run)
+
+    chip = chip_of(z, y_hi)
+
+    owned = OWNED if n == len(OWNED) else tuple(range(n))
+
+    away = [(dz, dy) for dz in range(depth) for dy in range(2) if dz or dy]
+    away.sort(key=lambda d: -min(d[0], depth - d[0]) - 4 * d[1])
+
+    def chips(action):
+        for dz, dy in away:
+            there, y = lax.rem(z + dz, depth), lax.rem(y_hi + dy, 2)
+            action(chip_of(there, y), {"items": (there * 2 + y) * 2 + core})
+
+    def users(action):
+        @pl.loop(1, n)
         def _(i):
-            p = start + stop - 1 - i if backwards else i
-
-            @pl.when(p != me)
-            def _():
-                action(p)
+            action(lax.rem(user + i, n))
 
     def send(src, dst, send_k, recv_sem, where):
         pltpu.make_async_remote_copy(
@@ -78,28 +83,28 @@
     def greet(where):
         pl.semaphore_signal(barrier, inc=1, device_id=where, device_id_type=MESH)
 
-    others(chip, 0, n, lambda p: greet(at_chip(p)))
-    others(user, 0, n, lambda p: greet({"users": p}))
+    chips(lambda c, where: greet(where))
+    users(lambda p: greet({"users": p}))
     greet(partner)
 
-    place = lax.broadcasted_iota(I32, (8, width), 0) * width + lax.broadcasted_iota(I32, (8, width), 1)
+    lane = lax.broadcasted_iota(I32, (1, width), 1)
     sub = lax.broadcasted_iota(I32, (slots, width), 0)
     for i in (4, 5, 6):
         loads[i].wait()
-    mrow = jnp.zeros((8, width), I32)
-    mcol = jnp.zeros((8, width), I32)
+    mrow = jnp.zeros((1, width), I32)
+    mcol = jnp.zeros((1, width), I32)
     colv = jnp.zeros((slots, width), I32)
     alive = count[0, 0]
     for t in range(slots):
         r, c = rows[0, 0, t], cols[0, 0, t]
         live = t < alive
-        mrow = jnp.where(place == chip * slots + t, jnp.where(live, r, -1), mrow)
-        mcol = jnp.where(place == user * slots + t, jnp.where(live, c, -1), mcol)
+        mrow = jnp.where(lane == lax.rem(chip * slots + t, width), jnp.where(live, r, -1), mrow)
+        mcol = jnp.where(lane == lax.rem(user * slots + t, width), jnp.where(live, c, -1), mcol)
         colv = jnp.where(sub == t, c, colv)
     meta_r_out[...] = mrow
     meta_c_out[...] = mcol
-    part(meta_r, chip, 8)[...] = mrow
-    part(meta_c, user, 8)[...] = mcol
+    meta_r[chip] = mrow
+    meta_c[user] = mcol
 
     loads[0].wait()
     hlen = hist.shape[1]
@@ -110,7 +115,7 @@
         h = hist[q : q + 1, :]
         block = lax.shift_right_logical(h, bits) == colw
         spot = (h & (width - 1)) == lane_id
-        hits[pl.ds(q, slots, stride=n), :] = dot(
+        hits[pl.ds(owned.index(q), slots, stride=n), :] = dot(
             jnp.where(block, 1.0, 0.0).astype(BF16), jnp.where(spot, 1.0, 0.0).astype(BF16), NT
         )
 
@@ -127,26 +132,26 @@
 
     pl.semaphore_wait(barrier, 2 * (n - 1) + 1)
 
-    def forth(p):
-        send(meta_r_out, part(meta_r, chip, 8), 1, sem.at[2], at_chip(p))
-        send(part(msg1, p), part(recv1, chip), 5, sem.at[6], at_chip(p))
-
-    others(chip, 0, n, forth, backwards=True)
+    def forth(c, where):
+        send(meta_r_out, meta_r.at[chip], 1, sem.at[2], where)
+        send(part(msg1, c), part(recv1, chip), 5, sem.at[6], where)
+
+    chips(forth)
     part(recv1, chip)[...] = part(msg1, chip)[...]
-    others(user, 0, n, lambda p: send(meta_c_out, part(meta_c, user, 8), 3, sem.at[4], {"users": p}))
-
-    def gathered(ref):
-        total = ref[0:8, :]
-        for i in range(1, n):
-            total = total + ref[8 * i : 8 * i + 8, :]
-        return total
-
-    wait(meta_r, 8 * (n - 1), 2)
-    ids = gathered(meta_r)
+    users(lambda p: send(meta_c_out, meta_c.at[user], 3, sem.at[4], {"users": p}))
+
+    def gathered(ref, k):
+        ids = jnp.zeros((1, width), I32)
+        for i in range(k * width // slots, min(n, -(-(k + 1) * width // slots))):
+            from_i = (lane >= i * slots - k * width) & (lane < (i + 1) * slots - k * width)
+            ids = jnp.where(from_i, ref[i], ids)
+        return ids
+
+    wait(meta_r, n - 1, 2)
     block = lax.broadcasted_iota(I32, (width, width), 0)
     for k in range(span // width):
         at = slice(k * width, (k + 1) * width)
-        hot = jnp.where(ids[k : k + 1, :] == block, 1.0, 0.0)
+        hot = jnp.where(gathered(meta_r, k) == block, 1.0, 0.0)
         pick_r[:, at] = hot[:user_blocks].astype(BF16)
         pick_rt[at, :] = hot.T.astype(BF16)
 
@@ -164,21 +169,14 @@
     high, low = halves(weights)
     back = pick_rt[:, :user_blocks]
     msg2[...] = dot(back, high) + dot(back, low)
-    mine = back_sem.at[chip // per]
-    others(chip, 0, n, lambda p: send(part(msg2, p), part(recv2, chip), 9, mine, at_chip(p)))
+    mine = back_sem.at[chip // run]
+    chips(lambda c, where: send(part(msg2, c), part(recv2, chip), 9, mine, where))
     part(recv2, chip)[...] = part(msg2, chip)[...]
 
-    wait(meta_c, 8 * (n - 1), 4)
-    ids = gathered(meta_c)
-    block = lax.broadcasted_iota(I32, (item_blocks, width), 0)
-    for k in range(span // width):
-        at = slice(k * width, (k + 1) * width)
-        pick_c[:, at] = jnp.where(ids[k : k + 1, :] == block, 1.0, 0.0).astype(BF16)
-
-    @pl.loop(0, GROUPS)
-    def _(g):
-        own = chip // per == g
-        for came, senders in ((own, per - 1), (jnp.logical_not(own), per)):
+    @pl.loop(0, 4)
+    def _(j):
+        g = lax.rem(z // run + lax.rem(j, 2), 2) * 2 + lax.rem(y_hi + j // 2, 2)
+        for came, senders in ((j == 0, run - 1), (j > 0, run)):
 
             @pl.when(came)
             def _():
@@ -186,22 +184,34 @@
                 pltpu.make_async_copy(piece, piece, back_sem.at[g]).wait()
 
         for t in range(slots):
-            spots = pl.ds(g * (per * slots) + t, per, stride=slots)
+            spots = pl.ds(g * (run * slots) + t, run, stride=slots)
             high, low = halves(recv2[spots, :])
             msg3[spots, :] = dot(high, vhi[t]) + dot(low, vhi[t]) + dot(high, vlo[t])
 
-        others(
-            user, g * per, (g + 1) * per,
-            lambda p: send(part(msg3, p), part(recv3, user), 11, sem.at[12], {"users": p}),
-        )
-
-    part(recv3, user)[...] = part(msg3, user)[...]
+        for m in range(run):
+            c, u = g * run + m, owned[m]
+            for k in range(1, 4):
+                u = jnp.where(g == k, owned[k * run + m], u)
+
+            @pl.when(u != user)
+            def _():
+                send(part(msg3, c), part(recv3, user), 11, sem.at[12], {"users": u})
+
+    own = 0
+    for c in range(1, n):
+        own = jnp.where(user == owned[c], c, own)
+    part(recv3, user)[...] = part(msg3, own)[...]
+    wait(meta_c, n - 1, 4)
+    block = lax.broadcasted_iota(I32, (item_blocks, width), 0)
+    for k in range(span // width):
+        at = slice(k * width, (k + 1) * width)
+        pick_c[:, at] = jnp.where(gathered(meta_c, k) == block, 1.0, 0.0).astype(BF16)
     wait(recv3, slots * (n - 1), 12)
     high, low = halves(recv3[...])
     out[...] = dot(pick_c[...], high) + dot(pick_c[...], low)
 
-    wait(meta_r, 8 * (n - 1), 1)
-    wait(meta_c, 8 * (n - 1), 3)
+    wait(meta_r, n - 1, 1)
+    wait(meta_c, n - 1, 3)
     wait(msg1, slots * (n - 1), 5)
     wait(msg2, slots * (n - 1), 9)
     wait(msg3, slots * (n - 1), 11)
@@ -234,28 +244,28 @@
             pltpu.VMEM((user_blocks, width), F32),
             pltpu.VMEM((user_blocks, width), F32),
             panel, panel, panel, panel,
-            pltpu.VMEM((8, width), I32),
-            pltpu.VMEM((8 * queries, width), I32),
-            pltpu.VMEM((8, width), I32),
-            pltpu.VMEM((8 * queries, width), I32),
+            pltpu.VMEM((1, width), I32),
+            pltpu.VMEM((queries, 1, width), I32),
+            pltpu.VMEM((1, width), I32),
+            pltpu.VMEM((queries, 1, width), I32),
             pltpu.VMEM((user_blocks, span), BF16),
             pltpu.VMEM((span, width), BF16),
             pltpu.VMEM((item_blocks, span), BF16),
             pltpu.SemaphoreType.DMA((7,)),
-            pltpu.SemaphoreType.DMA((GROUPS,)),
+            pltpu.SemaphoreType.DMA((4,)),
             pltpu.SemaphoreType.DMA((13,)),
         ],
         compiler_params=pltpu.CompilerParams(
-            collective_id=0, has_side_effects=True, vmem_limit_bytes=63 * 1024 * 1024
+            collective_id=0, has_side_effects=True, vmem_limit_bytes=32 * 1024 * 1024
         ),
         cost_estimate=pl.CostEstimate(flops=10**8, bytes_accessed=4 * 10**6, transcendentals=0),
-    )(
+    )(*[pltpu.with_memory_space_constraint(x, pltpu.HBM) for x in (
         histories,
         item_degree.reshape(item_blocks, width),
         user_degree.reshape(user_blocks, width),
         tile_values.reshape(slots, width, width),
-        tile_rows, tile_cols, tile_count,
-    )
+        tile_rows, tile_cols,
+    )], tile_count)
     return scores.reshape(1, item_blocks * width)
 
 

time: 45.5 us -> 40.8 us (0.90)
  the two profiles are of different devices: /device:TPU:24 before, /device:TPU:40 now
where the time goes in v4:
time: 40.8 us; the launch traced here: 40.6 us
  Pallas kernels  39.3 us (96%)
  local copies, waits for them, and re-layouts  0.66 us (2%)
  between operations  0.66 us (2%)
    pallas_call x1, Pallas kernels, body(): pl.pallas_call(functools.partial(kernel, slots, queries, user_blocks, ite...  39.3 us

profile of v4, /device:TPU:40, one launch (start us, length us, event | category | flops | bytes accessed | tf_op | source)
XLA Modules:
  0.0 40.6 jit_solution(10958693735152860006)
XLA Ops:
  0.7 39.3 %shard_map.73 = f32[256,128]{1,0:T(8,128)S(1)} custom-call(s32[16,256]{1,0:T(8,128)} %refs_0_.1, s32[256,128]{1,0:T(8,128)} %bitcast.6, s32[64,128]{1,0:T(8,128)} %bitcast.7, f32[24,128,128]{2,1,0:T(8,128)} %bitcast.5, s32[1,1,24]{2,1,0:T(1,128)} %refs_4_.1, s32[1,1,24]{2,1,0:T(1,128)} %refs_5_.1, s32[1,1]{1,0:T(1,128)S(6)} %copy.9.refs_6_), custom_call_target="tpu_custom_call" | custom-call | flops 100000000 | bytes 4000000 | tf_op jit(solution)/shard_map/pallas_call | solution.py:228
  39.9 0.7 %copy.10 = f32[1,32768]{1,0:T(1,128)} copy(f32[1,32768]{1,0:T(1,128)S(1)} %bitcast.4) | data formatting | bytes 262144

commit v5 on v4

--- a/solution.py
+++ b/solution.py
@@ -27,12 +27,15 @@
 OWNED = (0, 1, 4, 3, 8, 9, 11, 12, 2, 5, 7, 6, 13, 10, 15, 14)
 
 
+PIECE = 4
+
+
 def kernel(slots, queries, user_blocks, item_blocks, width, *refs):
     inputs, out, local = refs[:7], refs[7], refs[8:15]
     (
         vhi, vlo, hits, msg1, recv1, xsend, xrecv, msg2, recv2, msg3, recv3,
         meta_r_out, meta_r, meta_c_out, meta_c, pick_r, pick_rt, pick_c,
-        load_sem, back_sem, sem,
+        load_sem, vals_sem, back_sem, sem,
     ) = refs[15:]
     hist, ideg, udeg, vals, rows, cols, count = local
     n = queries
@@ -51,7 +54,7 @@
     owned = OWNED if n == len(OWNED) else tuple(range(n))
 
     away = [(dz, dy) for dz in range(depth) for dy in range(2) if dz or dy]
-    away.sort(key=lambda d: -min(d[0], depth - d[0]) - 4 * d[1])
+    away.sort(key=lambda d: -min(d[0], depth - d[0]) - 10 * d[1])
 
     def chips(action):
         for dz, dy in away:
@@ -76,9 +79,13 @@
         pltpu.make_async_copy(piece, piece, sem.at[k]).wait()
 
     barrier = pltpu.get_barrier_semaphore()
-    loads = [pltpu.make_async_copy(inputs[i], local[i], load_sem.at[i]) for i in range(7)]
-    for i in (4, 5, 6, 0, 1, 3, 2):
-        loads[i].start()
+    loads = {i: pltpu.make_async_copy(inputs[i], local[i], load_sem.at[i]) for i in (0, 1, 2, 4, 5, 6)}
+    pieces = []
+    for i in range(0, slots, PIECE):
+        here = pl.ds(i, PIECE)
+        pieces.append(pltpu.make_async_copy(inputs[3].at[here], vals.at[here], vals_sem.at[i // PIECE]))
+    for load in (loads[4], loads[5], loads[6], loads[0], loads[1], *pieces, loads[2]):
+        load.start()
 
     def greet(where):
         pl.semaphore_signal(barrier, inc=1, device_id=where, device_id_type=MESH)
@@ -120,9 +127,10 @@
         )
 
     loads[1].wait()
-    loads[3].wait()
 
     for t in range(slots):
+        if t % PIECE == 0:
+            pieces[t // PIECE].wait()
         degree = ideg[pl.ds(cols[0, 0, t], 1), :]
         high, low = halves(vals[t] * lax.rsqrt(degree.astype(F32)))
         vhi[t] = high
@@ -151,9 +159,7 @@
     block = lax.broadcasted_iota(I32, (width, width), 0)
     for k in range(span // width):
         at = slice(k * width, (k + 1) * width)
-        hot = jnp.where(gathered(meta_r, k) == block, 1.0, 0.0)
-        pick_r[:, at] = hot[:user_blocks].astype(BF16)
-        pick_rt[at, :] = hot.T.astype(BF16)
+        pick_r[:, at] = jnp.where(gathered(meta_r, k) == block[:user_blocks], 1.0, 0.0).astype(BF16)
 
     wait(recv1, slots * (n - 1), 6)
     high, low = halves(recv1[...])
@@ -163,8 +169,11 @@
         xsend, xrecv, sem.at[7], sem.at[8], device_id=partner, device_id_type=MESH
     )
     cross.start()
+    for k in range(span // width):
+        hot = jnp.where(gathered(meta_r, k) == block, 1.0, 0.0)
+        pick_rt[k * width : (k + 1) * width, :] = hot.T.astype(BF16)
+    loads[2].wait()
     cross.wait()
-    loads[2].wait()
     weights = (acc + xrecv[...]) / udeg[...].astype(F32)
     high, low = halves(weights)
     back = pick_rt[:, :user_blocks]
@@ -185,8 +194,11 @@
 
         for t in range(slots):
             spots = pl.ds(g * (run * slots) + t, run, stride=slots)
-            high, low = halves(recv2[spots, :])
-            msg3[spots, :] = dot(high, vhi[t]) + dot(low, vhi[t]) + dot(high, vlo[t])
+            x = recv2[spots, :]
+            high = x.astype(BF16).astype(F32)
+            x = jnp.concatenate([high, x - high], axis=0).astype(BF16)
+            y = dot(x, vhi[t]) + dot(x, vlo[t])
+            msg3[spots, :] = y[:run] + y[run:]
 
         for m in range(run):
             c, u = g * run + m, owned[m]
@@ -252,6 +264,7 @@
             pltpu.VMEM((span, width), BF16),
             pltpu.VMEM((item_blocks, span), BF16),
             pltpu.SemaphoreType.DMA((7,)),
+            pltpu.SemaphoreType.DMA((slots // PIECE,)),
             pltpu.SemaphoreType.DMA((4,)),
             pltpu.SemaphoreType.DMA((13,)),
         ],

time: 40.8 us -> 40.4 us (level)
  the two profiles are of different devices: /device:TPU:40 before, /device:TPU:24 now
where the time goes in v5:
time: 40.4 us; the launch traced here: 40.2 us
  Pallas kernels  38.9 us (96%)
  local copies, waits for them, and re-layouts  0.66 us (2%)
  between operations  0.66 us (2%)
    pallas_call x1, Pallas kernels, body(): pl.pallas_call(functools.partial(kernel, slots, queries, user_blocks, ite...  38.9 us

profile of v5, /device:TPU:24, one launch (start us, length us, event | category | flops | bytes accessed | tf_op | source)
XLA Modules:
  0.0 40.2 jit_solution(9152686081522388121)
XLA Ops:
  0.7 38.9 %shard_map.73 = f32[256,128]{1,0:T(8,128)S(1)} custom-call(s32[16,256]{1,0:T(8,128)} %refs_0_.1, s32[256,128]{1,0:T(8,128)} %bitcast.6, s32[64,128]{1,0:T(8,128)} %bitcast.7, f32[24,128,128]{2,1,0:T(8,128)} %bitcast.5, s32[1,1,24]{2,1,0:T(1,128)} %refs_4_.1, s32[1,1,24]{2,1,0:T(1,128)} %refs_5_.1, s32[1,1]{1,0:T(1,128)S(6)} %copy.9.refs_6_), custom_call_target="tpu_custom_call" | custom-call | flops 100000000 | bytes 4000000 | tf_op jit(solution)/shard_map/pallas_call | solution.py:240
  39.5 0.7 %copy.10 = f32[1,32768]{1,0:T(1,128)} copy(f32[1,32768]{1,0:T(1,128)S(1)} %bitcast.4) | data formatting | bytes 262144

commit v6 on v5

--- a/solution.py
+++ b/solution.py
@@ -25,6 +25,12 @@
 
 
 OWNED = (0, 1, 4, 3, 8, 9, 11, 12, 2, 5, 7, 6, 13, 10, 15, 14)
+
+
+def select(hot, x):
+    wide = x.shape[1]
+    y = dot(hot, jnp.concatenate(halves(x), axis=1))
+    return y[:, :wide] + y[:, wide:]
 
 
 PIECE = 4
@@ -162,8 +168,7 @@
         pick_r[:, at] = jnp.where(gathered(meta_r, k) == block[:user_blocks], 1.0, 0.0).astype(BF16)
 
     wait(recv1, slots * (n - 1), 6)
-    high, low = halves(recv1[...])
-    acc = dot(pick_r[...], high) + dot(pick_r[...], low)
+    acc = select(pick_r[...], recv1[...])
     xsend[...] = acc
     cross = pltpu.make_async_remote_copy(
         xsend, xrecv, sem.at[7], sem.at[8], device_id=partner, device_id_type=MESH
@@ -175,9 +180,7 @@
     loads[2].wait()
     cross.wait()
     weights = (acc + xrecv[...]) / udeg[...].astype(F32)
-    high, low = halves(weights)
-    back = pick_rt[:, :user_blocks]
-    msg2[...] = dot(back, high) + dot(back, low)
+    msg2[...] = select(pick_rt[:, :user_blocks], weights)
     mine = back_sem.at[chip // run]
     chips(lambda c, where: send(part(msg2, c), part(recv2, chip), 9, mine, where))
     part(recv2, chip)[...] = part(msg2, chip)[...]
@@ -219,8 +222,7 @@
         at = slice(k * width, (k + 1) * width)
         pick_c[:, at] = jnp.where(gathered(meta_c, k) == block, 1.0, 0.0).astype(BF16)
     wait(recv3, slots * (n - 1), 12)
-    high, low = halves(recv3[...])
-    out[...] = dot(pick_c[...], high) + dot(pick_c[...], low)
+    out[...] = select(pick_c[...], recv3[...])
 
     wait(meta_r, n - 1, 1)
     wait(meta_c, n - 1, 3)

time: 40.4 us -> 40.4 us (level)
  no operation moved by 1% of the time
where the time goes in v6:
time: 40.4 us; the launch traced here: 40.2 us
  Pallas kernels  38.9 us (96%)
  local copies, waits for them, and re-layouts  0.66 us (2%)
  between operations  0.66 us (2%)
    pallas_call x1, Pallas kernels, body(): pl.pallas_call(functools.partial(kernel, slots, queries, user_blocks, ite...  38.9 us

profile of v6, /device:TPU:24, one launch (start us, length us, event | category | flops | bytes accessed | tf_op | source)
XLA Modules:
  0.0 40.2 jit_solution(17637041317895272845)
XLA Ops:
  0.7 38.9 %shard_map.73 = f32[256,128]{1,0:T(8,128)S(1)} custom-call(s32[16,256]{1,0:T(8,128)} %refs_0_.1, s32[256,128]{1,0:T(8,128)} %bitcast.6, s32[64,128]{1,0:T(8,128)} %bitcast.7, f32[24,128,128]{2,1,0:T(8,128)} %bitcast.5, s32[1,1,24]{2,1,0:T(1,128)} %refs_4_.1, s32[1,1,24]{2,1,0:T(1,128)} %refs_5_.1, s32[1,1]{1,0:T(1,128)S(6)} %copy.9.refs_6_), custom_call_target="tpu_custom_call" | custom-call | flops 100000000 | bytes 4000000 | tf_op jit(solution)/shard_map/pallas_call | solution.py:242
  39.6 0.7 %copy.10 = f32[1,32768]{1,0:T(1,128)} copy(f32[1,32768]{1,0:T(1,128)S(1)} %bitcast.4) | data formatting | bytes 262144

commit v7 on v6

--- a/solution.py
+++ b/solution.py
@@ -152,7 +152,6 @@
 
     chips(forth)
     part(recv1, chip)[...] = part(msg1, chip)[...]
-    users(lambda p: send(meta_c_out, meta_c.at[user], 3, sem.at[4], {"users": p}))
 
     def gathered(ref, k):
         ids = jnp.zeros((1, width), I32)
@@ -184,6 +183,8 @@
     mine = back_sem.at[chip // run]
     chips(lambda c, where: send(part(msg2, c), part(recv2, chip), 9, mine, where))
     part(recv2, chip)[...] = part(msg2, chip)[...]
+
+    users(lambda p: send(meta_c_out, meta_c.at[user], 3, sem.at[4], {"users": p}))
 
     @pl.loop(0, 4)
     def _(j):

time: 40.4 us -> 40.4 us (level)
  no operation moved by 1% of the time
where the time goes in v7:
time: 40.4 us; the launch traced here: 40.3 us
  Pallas kernels  39 us (97%)
  local copies, waits for them, and re-layouts  0.66 us (2%)
  between operations  0.66 us (2%)
    pallas_call x1, Pallas kernels, body(): pl.pallas_call(functools.partial(kernel, slots, queries, user_blocks, ite...  39 us

profile of v7, /device:TPU:24, one launch (start us, length us, event | category | flops | bytes accessed | tf_op | source)
XLA Modules:
  0.0 40.3 jit_solution(18154477343114801192)
XLA Ops:
  0.7 39.0 %shard_map.73 = f32[256,128]{1,0:T(8,128)S(1)} custom-call(s32[16,256]{1,0:T(8,128)} %refs_0_.1, s32[256,128]{1,0:T(8,128)} %bitcast.6, s32[64,128]{1,0:T(8,128)} %bitcast.7, f32[24,128,128]{2,1,0:T(8,128)} %bitcast.5, s32[1,1,24]{2,1,0:T(1,128)} %refs_4_.1, s32[1,1,24]{2,1,0:T(1,128)} %refs_5_.1, s32[1,1]{1,0:T(1,128)S(6)} %copy.9.refs_6_), custom_call_target="tpu_custom_call" | custom-call | flops 100000000 | bytes 4000000 | tf_op jit(solution)/shard_map/pallas_call | solution.py:243
  39.6 0.7 %copy.10 = f32[1,32768]{1,0:T(1,128)} copy(f32[1,32768]{1,0:T(1,128)S(1)} %bitcast.4) | data formatting | bytes 262144
